TPU v7x, 32 devices: a whole 2x2x4 slice. The times are simulated.
32 devices in a mesh: groups: 2 (over x), ctx: 16 (over z, y, core).
Axes of the slice: x: 2, y: 2, z: 4, core: 2. Of those that a mesh axis runs over, the one named last changes fastest.
Arguments:
- query: bfloat16 [4096, 1536], P(('groups', 'ctx')), parts along dimension 0, may hold values from -5 to 5
- key_rows: bfloat16 [4096, 1536], P(('groups', 'ctx')), parts along dimension 0, may hold values from -5 to 5
- value: bfloat16 [4096, 1536], P(('groups', 'ctx')), parts along dimension 0, may hold values from -6 to 6
- grad_out: bfloat16 [4096, 1536], P(('groups', 'ctx')), parts along dimension 0, may hold values from -6 to 6
- kv_slots: int32 [16, 18], replicated, may hold values from -1 to 15, as said below
Outputs:
- out: bfloat16 [4096, 1536], P(('groups', 'ctx')), parts along dimension 0
- grad_query: bfloat16 [4096, 1536], P(('groups', 'ctx')), parts along dimension 0
- grad_key: bfloat16 [4096, 1536], P(('groups', 'ctx')), parts along dimension 0
- grad_value: bfloat16 [4096, 1536], P(('groups', 'ctx')), parts along dimension 0
There are 2 independent parts, one for each index of `groups`. A program takes and returns all parts, laid end to end along the dimension named above; an argument that names none is the same for every part. Nothing has to cross between parts.
Inputs may be any that keep to these rules, and one draw needn't show every extreme that they name: `kv_slots`: blocks are the tiles of two time planes of 4 x 2 tiles in raster order (plane, row, column). The row of block b lists, in a drawn order, b itself and a drawn subset of the blocks whose tile lies in either plane within one row and one column of b's tile; -1 fills the other entries. No block is listed twice in a row.
All inputs are finite; a program needn't handle non-finite values.
Results may differ from a plain program's by a relative error of at most 0.0065.
The roundings to bfloat16 on the way count: a program that leaves them out, or rounds other values in their place, can miss the bound.
Values may be sent and summed in bfloat16 or wider, within the bound.
A program may use at most 128 MiB of HBM per device.

v0:
```python
import jax
import jax.numpy as jnp
from jax import lax
from jax.sharding import PartitionSpec as P

HEADS = 12
HEAD = 128
BLOCK = 128
TILE_H = 4


head_batch = 4
masked_score = -1e30


def from_behind(value, axis, by):
    count = lax.axis_size(axis)
    return lax.ppermute(value, axis, [(i, (i + by) % count) for i in range(count)])


def neighbour_offsets(devices, blocks, tile_width):
    plane_size = TILE_H * tile_width
    total_slots = devices * blocks
    offset_set = set()
    for plane_step in (0, 1):
        for row_step in (-1, 0, 1):
            for col_step in (-1, 0, 1):
                offset = (plane_step * plane_size + row_step * tile_width + col_step) % total_slots
                target = offset % total_slots // blocks
                if target > devices // 2:
                    target = target - devices
                if target != 0:
                    offset_set.add(target)
    return offset_set


def split_heads(tensor):
    return tensor.reshape(
        tensor.shape[0], HEADS // head_batch, head_batch, tensor.shape[1] // HEADS
    )


def pick_group(tensor, group_index):
    return lax.dynamic_index_in_dim(tensor, group_index, 1, keepdims=False)


def join_heads(stacked):
    return jnp.moveaxis(stacked, 0, 1).reshape(stacked.shape[1], -1)


def apply_mask(scores, block_mask):
    heads_here, row_total, col_total = scores.shape
    row_blocks, col_blocks = block_mask.shape
    shaped = scores.reshape(
        heads_here, row_blocks, row_total // row_blocks, col_blocks, col_total // col_blocks
    )
    shaped = jnp.where(block_mask[None, :, None, :, None], shaped, masked_score)
    return shaped.reshape(heads_here, row_total, col_total)


def forward_group(group_index, queries, keys, values, allowed, scaling):
    query_part = pick_group(queries, group_index)
    key_part = pick_group(keys, group_index)
    value_part = pick_group(values, group_index)
    scores = (
        jnp.einsum("qhd,khd->hqk", query_part, key_part, preferred_element_type=jnp.float32)
        * scaling
    )
    scores = apply_mask(scores, allowed)
    peak_score = jnp.max(scores, axis=2, keepdims=True)
    denominator = jnp.sum(jnp.exp(scores - peak_score), axis=2, keepdims=True)
    log_norm = peak_score + jnp.log(denominator)
    weights = jnp.exp(scores - log_norm).astype(jnp.bfloat16)
    mixed_rows = jnp.einsum("hqk,khd->qhd", weights, value_part, preferred_element_type=jnp.float32)
    return (mixed_rows, log_norm[:, :, 0])


def query_group(
    group_index, queries, keys, values, gradients, log_split, delta_split, allowed, scaling
):
    query_part = pick_group(queries, group_index)
    key_part = pick_group(keys, group_index)
    value_part = pick_group(values, group_index)
    grad_part = pick_group(gradients, group_index)
    log_part = jnp.transpose(pick_group(log_split, group_index))
    delta_part = jnp.transpose(pick_group(delta_split, group_index))
    scores = (
        jnp.einsum("qhd,khd->hqk", query_part, key_part, preferred_element_type=jnp.float32)
        * scaling
    )
    scores = apply_mask(scores, allowed)
    weights = jnp.exp(scores - log_part[:, :, None])
    grad_probs = jnp.einsum(
        "qhd,khd->hqk", grad_part, value_part, preferred_element_type=jnp.float32
    )
    grad_scores = (weights * (grad_probs - delta_part[:, :, None])).astype(jnp.bfloat16)
    return (
        jnp.einsum("hqk,khd->qhd", grad_scores, key_part, preferred_element_type=jnp.float32)
        * scaling
    )


def key_group(
    group_index, keys, values, queries, gradients, log_split, delta_split, back_mask, scaling
):
    key_part = pick_group(keys, group_index)
    value_part = pick_group(values, group_index)
    query_part = pick_group(queries, group_index)
    grad_part = pick_group(gradients, group_index)
    log_part = jnp.transpose(pick_group(log_split, group_index))
    delta_part = jnp.transpose(pick_group(delta_split, group_index))
    scores = (
        jnp.einsum("khd,chd->hkc", key_part, query_part, preferred_element_type=jnp.float32)
        * scaling
    )
    scores = apply_mask(scores, back_mask)
    weights = jnp.exp(scores - log_part[:, None, :])
    grad_probs = jnp.einsum(
        "khd,chd->hkc", value_part, grad_part, preferred_element_type=jnp.float32
    )
    grad_scores = (weights * (grad_probs - delta_part[:, None, :])).astype(jnp.bfloat16)
    grad_values = jnp.einsum(
        "hkc,chd->khd", weights.astype(jnp.bfloat16), grad_part, preferred_element_type=jnp.float32
    )
    grad_keys = (
        jnp.einsum("hkc,chd->khd", grad_scores, query_part, preferred_element_type=jnp.float32)
        * scaling
    )
    return (grad_keys, grad_values)


def body(query, key_rows, value, grad_out, kv_slots):
    devices = lax.axis_size("ctx")
    device_index = lax.axis_index("ctx")
    row_count = query.shape[0]
    blocks = row_count // BLOCK
    tile_width = devices * blocks // (2 * TILE_H)
    offset_set = neighbour_offsets(devices, blocks, tile_width)
    visit_order = sorted(offset_set)
    distances = [0] + visit_order
    local_slots = jnp.arange(blocks, dtype=jnp.int32)
    cand_slots = jnp.concatenate(
        [(device_index + distance) % devices * blocks + local_slots for distance in distances]
    ).astype(jnp.int32)
    own_blocks = device_index * blocks + local_slots
    own_lists = lax.dynamic_slice_in_dim(kv_slots, device_index * blocks, blocks, 0)
    allowed = jnp.any(own_lists[:, :, None] == cand_slots[None, None, :], axis=1)
    cand_lists = jnp.take(kv_slots, cand_slots, axis=0)
    back_mask = jnp.any(cand_lists[None, :, :] == own_blocks[:, None, None], axis=2)
    scaling = HEAD ** (-0.5)
    groups = HEADS // head_batch
    group_ids = jnp.arange(groups)
    arrived = [from_behind((key_rows, value), "ctx", -distance) for distance in visit_order]
    cand_keys = split_heads(jnp.concatenate([key_rows] + [item[0] for item in arrived], axis=0))
    cand_values = split_heads(jnp.concatenate([value] + [item[1] for item in arrived], axis=0))
    queries = split_heads(query)
    mixed_all, norm_all = lax.map(
        lambda group_index: forward_group(
            group_index, queries, cand_keys, cand_values, allowed, scaling
        ),
        group_ids,
    )
    out = join_heads(mixed_all).astype(jnp.bfloat16)
    log_rows = jnp.transpose(norm_all.reshape(HEADS, row_count))
    delta_rows = jnp.sum(
        (grad_out.astype(jnp.float32) * out.astype(jnp.float32)).reshape(row_count, HEADS, -1),
        axis=2,
    )
    gradients = split_heads(grad_out)
    log_split = log_rows.reshape(row_count, groups, head_batch)
    delta_split = delta_rows.reshape(row_count, groups, head_batch)
    query_terms = lax.map(
        lambda group_index: query_group(
            group_index,
            queries,
            cand_keys,
            cand_values,
            gradients,
            log_split,
            delta_split,
            allowed,
            scaling,
        ),
        group_ids,
    )
    grad_query = join_heads(query_terms).astype(jnp.bfloat16)
    returned = [from_behind((query, grad_out), "ctx", -distance) for distance in visit_order]
    cand_queries = jnp.concatenate([query] + [item[0] for item in returned], axis=0)
    cand_grads = jnp.concatenate([grad_out] + [item[1] for item in returned], axis=0)
    row_terms = [from_behind((log_rows, delta_rows), "ctx", -distance) for distance in visit_order]
    cand_log = jnp.concatenate([log_rows] + [item[0] for item in row_terms], axis=0).reshape(
        -1, groups, head_batch
    )
    cand_delta = jnp.concatenate([delta_rows] + [item[1] for item in row_terms], axis=0).reshape(
        -1, groups, head_batch
    )
    own_keys = split_heads(key_rows)
    own_values = split_heads(value)
    split_queries = split_heads(cand_queries)
    split_grads = split_heads(cand_grads)
    key_terms, value_terms = lax.map(
        lambda group_index: key_group(
            group_index,
            own_keys,
            own_values,
            split_queries,
            split_grads,
            cand_log,
            cand_delta,
            back_mask,
            scaling,
        ),
        group_ids,
    )
    grad_key = join_heads(key_terms).astype(jnp.bfloat16)
    grad_value = join_heads(value_terms).astype(jnp.bfloat16)
    return (out, grad_query, grad_key, grad_value)


def solution(mesh):
    placed = (
        P(("groups", "ctx"), None),
        P(("groups", "ctx"), None),
        P(("groups", "ctx"), None),
        P(("groups", "ctx"), None),
        P(),
    )
    return jax.shard_map(
        body,
        mesh=mesh,
        in_specs=placed,
        out_specs=(
            P(("groups", "ctx"), None),
            P(("groups", "ctx"), None),
            P(("groups", "ctx"), None),
            P(("groups", "ctx"), None),
        ),
        check_vma=False,
    )
```

profile of v0, /device:TPU:15, one launch (start us, length us, event | category | flops | bytes accessed | tf_op | source)
XLA Modules:
  0.0 701.1 jit_solution(9705418312084618958)
XLA Ops:
  21.0 60.1 %collective-permute-done.13 = bf16[128,1536]{0,1:T(8,128)(2,1)} collective-permute-done((bf16[128,1536]{0,1:T(8,128)(2,1)S(1)}, bf16[128,1536]{0,1:T(8,128)(2,1)}, u32[]{:S(2)}, u32[]{:S(2)}) %collective-permute-start.13) | collective-permute-done | bytes 393248 | tf_op jit(solution)/shard_map/ppermute | solution.py:18
  82.9 6.6 collective-permute-done.14
  90.3 7.6 %collective-permute-done.15 = bf16[128,1536]{0,1:T(8,128)(2,1)S(1)} collective-permute-done((bf16[128,1536]{0,1:T(8,128)(2,1)S(1)}, bf16[128,1536]{0,1:T(8,128)(2,1)S(1)}, u32[]{:S(2)}, u32[]{:S(2)}) %collective-permute-start.15) | collective-permute-done | bytes 393248 | tf_op jit(solution)/shard_map/ppermute | solution.py:18
  98.7 7.6 %collective-permute-done.16 = bf16[128,1536]{0,1:T(8,128)(2,1)S(1)} collective-permute-done((bf16[128,1536]{0,1:T(8,128)(2,1)S(1)}, bf16[128,1536]{0,1:T(8,128)(2,1)S(1)}, u32[]{:S(2)}, u32[]{:S(2)}) %collective-permute-start.16) | collective-permute-done | bytes 393248 | tf_op jit(solution)/shard_map/ppermute | solution.py:18
  107.1 7.6 %collective-permute-done.17 = bf16[128,1536]{0,1:T(8,128)(2,1)S(1)} collective-permute-done((bf16[128,1536]{0,1:T(8,128)(2,1)S(1)}, bf16[128,1536]{0,1:T(8,128)(2,1)S(1)}, u32[]{:S(2)}, u32[]{:S(2)}) %collective-permute-start.17) | collective-permute-done | bytes 393248 | tf_op jit(solution)/shard_map/ppermute | solution.py:18
  131.0 7.5 %collective-permute-start.22 = (bf16[128,1536]{0,1:T(8,128)(2,1)S(1)}, bf16[128,1536]{0,1:T(8,128)(2,1)S(1)}, u32[]{:S(2)}, u32[]{:S(2)}) collective-permute-start(bf16[128,1536]{0,1:T(8,128)(2,1)S(1)} %copy.104), channel_id=1, source_target_pairs={{0,11},{1,12},{2,13},{3,14},{4,15},{5,0},{6,1},{7,2},{8,3},{9,4},{... | collective-permute-start | bytes 1179656 | tf_op jit(solution)/shard_map/ppermute | solution.py:18
  159.7 30.0 %collective-permute-start.25 = (bf16[128,1536]{0,1:T(8,128)(2,1)S(1)}, bf16[128,1536]{0,1:T(8,128)(2,1)S(1)}, u32[]{:S(2)}, u32[]{:S(2)}) collective-permute-start(bf16[128,1536]{0,1:T(8,128)(2,1)S(1)} %copy.104), channel_id=1, source_target_pairs={{0,8},{1,9},{2,10},{3,11},{4,12},{5,13},{6,14},{7,15},{8,0},{9,1},... | collective-permute-start | bytes 1179656 | tf_op jit(solution)/shard_map/ppermute | solution.py:18
  191.4 7.4 %collective-permute-done.25 = bf16[128,1536]{0,1:T(8,128)(2,1)S(1)} collective-permute-done((bf16[128,1536]{0,1:T(8,128)(2,1)S(1)}, bf16[128,1536]{0,1:T(8,128)(2,1)S(1)}, u32[]{:S(2)}, u32[]{:S(2)}) %collective-permute-start.25) | collective-permute-done | bytes 393248 | tf_op jit(solution)/shard_map/ppermute | solution.py:18
  200.6 8.3 %copy.106 = bf16[1792,3,4,128]{3,0,2,1:T(8,128)(2,1)} copy(bf16[1792,3,4,128]{0,3,2,1:T(8,128)(2,1)} %bitcast.272) | data formatting | bytes 11010048 | tf_op jit(solution)/shard_map/while | solution.py:157
  208.8 9.3 %collective-permute-start.5 = (bf16[128,1536]{0,1:T(8,128)(2,1)S(1)}, bf16[128,1536]{0,1:T(8,128)(2,1)S(1)}, u32[]{:S(2)}, u32[]{:S(2)}) collective-permute-start(bf16[128,1536]{0,1:T(8,128)(2,1)S(1)} %copy.89), channel_id=1, source_target_pairs={{0,1},{1,2},{2,3},{3,4},{4,5},{5,6},{6,7},{7,8},{8,9},{9,10},{10,1... | collective-permute-start | bytes 1179656 | tf_op jit(solution)/shard_map/ppermute | solution.py:18
  231.2 17.0 %collective-permute-start.10 = (bf16[128,1536]{0,1:T(8,128)(2,1)S(1)}, bf16[128,1536]{0,1:T(8,128)(2,1)S(1)}, u32[]{:S(2)}, u32[]{:S(2)}) collective-permute-start(bf16[128,1536]{0,1:T(8,128)(2,1)S(1)} %copy.89), channel_id=1, source_target_pairs={{0,10},{1,11},{2,12},{3,13},{4,14},{5,15},{6,0},{7,1},{8,2},{9,3},... | collective-permute-start | bytes 1179656 | tf_op jit(solution)/shard_map/ppermute | solution.py:18
  271.2 22.8 %collective-permute-start.29 = (bf16[128,1536]{0,1:T(8,128)(2,1)S(1)}, bf16[128,1536]{0,1:T(8,128)(2,1)}, u32[]{:S(2)}, u32[]{:S(2)}) collective-permute-start(bf16[128,1536]{0,1:T(8,128)(2,1)S(1)} %copy.90), channel_id=1, source_target_pairs={{0,3},{1,4},{2,5},{3,6},{4,7},{5,8},{6,9},{7,10},{8,11},{9,12},{10... | collective-permute-start | bytes 1179656 | tf_op jit(solution)/shard_map/ppermute | solution.py:18
  294.9 40.4 %collective-permute-start.30 = (bf16[128,1536]{0,1:T(8,128)(2,1)S(1)}, bf16[128,1536]{0,1:T(8,128)(2,1)}, u32[]{:S(2)}, u32[]{:S(2)}) collective-permute-start(bf16[128,1536]{0,1:T(8,128)(2,1)S(1)} %copy.90), channel_id=1, source_target_pairs={{0,2},{1,3},{2,4},{3,5},{4,6},{5,7},{6,8},{7,9},{8,10},{9,11},{10,... | collective-permute-start | bytes 1179656 | tf_op jit(solution)/shard_map/ppermute | solution.py:18
  336.1 25.4 %while.34 = (s32[]{:T(128)}, bf16[3,128,4,128]{1,3,2,0:T(8,128)(2,1)S(1)}, f32[3,4,128]{2,1,0:T(4,128)}, s32[3]{0:T(128)S(1)}, bf16[1792,3,4,128]{0,3,2,1:T(8,12...) while((s32[]{:T(128)}, ...), condition=%wide.region_4.5_spmd, body=%wide.region_1.4_spmd.sunk | while | flops 476184064 | bytes 15094717 | solution.py:157
  363.6 36.8 %while.35 = (s32[]{:T(128)}, bf16[3,128,4,128]{1,3,2,0:T(8,128)(2,1)S(1)}, s32[3]{0:T(128)S(1)}, bf16[1792,3,4,128]{3,0,2,1:T(8,128)(2,1)}, pred[1,14]{1,0:T(4,1...) while((s32[]{:T(128)}, ...), condition=%wide.region_7.8_spmd, body=%wide.region_6.7_spmd.sunk | while | flops 710213632 | bytes 13388825 | solution.py:172
  425.6 9.6 %collective-permute-done.34 = bf16[128,1536]{0,1:T(8,128)(2,1)S(1)} collective-permute-done((bf16[128,1536]{0,1:T(8,128)(2,1)S(1)}, bf16[128,1536]{0,1:T(8,128)(2,1)S(1)}, u32[]{:S(2)}, u32[]{:S(2)}) %collective-permute-start.34) | collective-permute-done | bytes 393248 | tf_op jit(solution)/shard_map/ppermute | solution.py:18
  448.2 30.7 %collective-permute-start.55 = (bf16[128,1536]{0,1:T(8,128)(2,1)S(1)}, bf16[128,1536]{0,1:T(8,128)(2,1)S(1)}, u32[]{:S(2)}, u32[]{:S(2)}) collective-permute-start(bf16[128,1536]{0,1:T(8,128)(2,1)S(1)} %bitcast.279), channel_id=1, source_target_pairs={{0,3},{1,4},{2,5},{3,6},{4,7},{5,8},{6,9},{7,10},{8,11},{9,12},{10... | collective-permute-start | bytes 1179656 | tf_op jit(solution)/shard_map/ppermute | solution.py:18
  479.7 38.5 %collective-permute-start.56 = (bf16[128,1536]{0,1:T(8,128)(2,1)S(1)}, bf16[128,1536]{0,1:T(8,128)(2,1)S(1)}, u32[]{:S(2)}, u32[]{:S(2)}) collective-permute-start(bf16[128,1536]{0,1:T(8,128)(2,1)S(1)} %bitcast.280), channel_id=1, source_target_pairs={{0,2},{1,3},{2,4},{3,5},{4,6},{5,7},{6,8},{7,9},{8,10},{9,11},{10,... | collective-permute-start | bytes 1179656 | tf_op jit(solution)/shard_map/ppermute | solution.py:18
  530.6 20.8 %collective-permute-start.61 = (bf16[128,1536]{0,1:T(8,128)(2,1)S(1)}, bf16[128,1536]{0,1:T(8,128)(2,1)S(1)}, u32[]{:S(2)}, u32[]{:S(2)}) collective-permute-start(bf16[128,1536]{0,1:T(8,128)(2,1)S(1)} %bitcast.285), channel_id=1, source_target_pairs={{0,11},{1,12},{2,13},{3,14},{4,15},{5,0},{6,1},{7,2},{8,3},{9,4},{... | collective-permute-start | bytes 1179656 | tf_op jit(solution)/shard_map/ppermute | solution.py:18
  553.1 7.0 %collective-permute-start.63 = (bf16[128,1536]{0,1:T(8,128)(2,1)S(1)}, bf16[128,1536]{0,1:T(8,128)(2,1)S(1)}, u32[]{:S(2)}, u32[]{:S(2)}) collective-permute-start(bf16[128,1536]{0,1:T(8,128)(2,1)S(1)} %bitcast.287), channel_id=1, source_target_pairs={{0,9},{1,10},{2,11},{3,12},{4,13},{5,14},{6,15},{7,0},{8,1},{9,2},... | collective-permute-start | bytes 1179656 | tf_op jit(solution)/shard_map/ppermute | solution.py:18
  577.2 24.2 %collective-permute-start.42 = (f32[128,12]{0,1:T(8,128)S(1)}, f32[128,12]{0,1:T(8,128)S(1)}, u32[]{:S(2)}, u32[]{:S(2)}) collective-permute-start(f32[128,12]{0,1:T(8,128)S(1)} %bitcast.299), channel_id=1, source_target_pairs={{0,3},{1,4},{2,5},{3,6},{4,7},{5,8},{6,9},{7,10},{8,11},{9,12},{10... | collective-permute-start | bytes 18440 | tf_op jit(solution)/shard_map/ppermute | solution.py:18
  602.2 8.8 %collective-permute-start.43 = (f32[128,12]{0,1:T(8,128)S(1)}, f32[128,12]{0,1:T(8,128)S(1)}, u32[]{:S(2)}, u32[]{:S(2)}) collective-permute-start(f32[128,12]{0,1:T(8,128)S(1)} %bitcast.300), channel_id=1, source_target_pairs={{0,2},{1,3},{2,4},{3,5},{4,6},{5,7},{6,8},{7,9},{8,10},{9,11},{10,... | collective-permute-start | bytes 18440 | tf_op jit(solution)/shard_map/ppermute | solution.py:18
  613.7 7.8 %collective-permute-start.44 = (f32[128,12]{0,1:T(8,128)S(1)}, f32[128,12]{0,1:T(8,128)S(1)}, u32[]{:S(2)}, u32[]{:S(2)}) collective-permute-start(f32[128,12]{0,1:T(8,128)S(1)} %bitcast.301), channel_id=1, source_target_pairs={{0,1},{1,2},{2,3},{3,4},{4,5},{5,6},{6,7},{7,8},{8,9},{9,10},{10,1... | collective-permute-start | bytes 18440 | tf_op jit(solution)/shard_map/ppermute | solution.py:18
  655.3 43.9 %while.36 = (s32[]{:T(128)}, bf16[3,128,4,128]{1,3,2,0:T(8,128)(2,1)S(1)}, bf16[3,128,4,128]{1,3,2,0:T(8,128)(2,1)S(1)}, s32[3]{0:T(128)S(1)}, bf16[1792,3,4,128...) while((s32[]{:T(128)}, ...), condition=%wide.region_10.11_spmd, body=%wide.region_9.10_spmd.sunk | while | flops 946012160 | bytes 19315668 | solution.py:201
  (318 shorter events, 302.9 us)
Async XLA Ops:
  1.9 207.0 %collective-permute-start = (bf16[128,1536]{0,1:T(8,128)(2,1)S(1)}, bf16[128,1536]{0,1:T(8,128)(2,1)S(1)}, u32[]{:S(2)}, u32[]{:S(2)}) collective-permute-start(bf16[128,1536]{0,1:T(8,128)(2,1)S(1)} %copy.89), channel_id=1, source_target_pairs={{0,7},{1,8},{2,9},{3,10},{4,11},{5,12},{6,13},{7,14},{8,15},{9,0},... | collective-permute-start | bytes 1179656 | tf_op jit(solution)/shard_map/ppermute | solution.py:18
  4.8 214.1 %collective-permute-start.1 = (bf16[128,1536]{0,1:T(8,128)(2,1)S(1)}, bf16[128,1536]{0,1:T(8,128)(2,1)S(1)}, u32[]{:S(2)}, u32[]{:S(2)}) collective-permute-start(bf16[128,1536]{0,1:T(8,128)(2,1)S(1)} %copy.89), channel_id=1, source_target_pairs={{0,6},{1,7},{2,8},{3,9},{4,10},{5,11},{6,12},{7,13},{8,14},{9,15},... | collective-permute-start | bytes 1179656 | tf_op jit(solution)/shard_map/ppermute | solution.py:18
  4.8 215.0 %collective-permute-start.2 = (bf16[128,1536]{0,1:T(8,128)(2,1)S(1)}, bf16[128,1536]{0,1:T(8,128)(2,1)S(1)}, u32[]{:S(2)}, u32[]{:S(2)}) collective-permute-start(bf16[128,1536]{0,1:T(8,128)(2,1)S(1)} %copy.89), channel_id=1, source_target_pairs={{0,5},{1,6},{2,7},{3,8},{4,9},{5,10},{6,11},{7,12},{8,13},{9,14},{... | collective-permute-start | bytes 1179656 | tf_op jit(solution)/shard_map/ppermute | solution.py:18
  9.1 71.9 %collective-permute-start.13 = (bf16[128,1536]{0,1:T(8,128)(2,1)S(1)}, bf16[128,1536]{0,1:T(8,128)(2,1)}, u32[]{:S(2)}, u32[]{:S(2)}) collective-permute-start(bf16[128,1536]{0,1:T(8,128)(2,1)S(1)} %copy.104), channel_id=1, source_target_pairs={{0,7},{1,8},{2,9},{3,10},{4,11},{5,12},{6,13},{7,14},{8,15},{9,0},... | collective-permute-start | bytes 1179656 | tf_op jit(solution)/shard_map/ppermute | solution.py:18
  9.2 80.3 %collective-permute-start.14 = (bf16[128,1536]{0,1:T(8,128)(2,1)S(1)}, bf16[128,1536]{0,1:T(8,128)(2,1)S(1)}, u32[]{:S(2)}, u32[]{:S(2)}) collective-permute-start(bf16[128,1536]{0,1:T(8,128)(2,1)S(1)} %copy.104), channel_id=1, source_target_pairs={{0,6},{1,7},{2,8},{3,9},{4,10},{5,11},{6,12},{7,13},{8,14},{9,15},... | collective-permute-start | bytes 1179656 | tf_op jit(solution)/shard_map/ppermute | solution.py:18
  150.5 40.2 %collective-permute-start.24 = (bf16[128,1536]{0,1:T(8,128)(2,1)S(1)}, bf16[128,1536]{0,1:T(8,128)(2,1)S(1)}, u32[]{:S(2)}, u32[]{:S(2)}) collective-permute-start(bf16[128,1536]{0,1:T(8,128)(2,1)S(1)} %copy.104), channel_id=1, source_target_pairs={{0,9},{1,10},{2,11},{3,12},{4,13},{5,14},{6,15},{7,0},{8,1},{9,2},... | collective-permute-start | bytes 1179656 | tf_op jit(solution)/shard_map/ppermute | solution.py:18
  159.7 39.1 %collective-permute-start.25 = (bf16[128,1536]{0,1:T(8,128)(2,1)S(1)}, bf16[128,1536]{0,1:T(8,128)(2,1)S(1)}, u32[]{:S(2)}, u32[]{:S(2)}) collective-permute-start(bf16[128,1536]{0,1:T(8,128)(2,1)S(1)} %copy.104), channel_id=1, source_target_pairs={{0,8},{1,9},{2,10},{3,11},{4,12},{5,13},{6,14},{7,15},{8,0},{9,1},... | collective-permute-start | bytes 1179656 | tf_op jit(solution)/shard_map/ppermute | solution.py:18
  255.7 39.2 %collective-permute-start.12 = (bf16[128,1536]{0,1:T(8,128)(2,1)S(1)}, bf16[128,1536]{0,1:T(8,128)(2,1)S(1)}, u32[]{:S(2)}, u32[]{:S(2)}) collective-permute-start(bf16[128,1536]{0,1:T(8,128)(2,1)S(1)} %copy.89), channel_id=1, source_target_pairs={{0,8},{1,9},{2,10},{3,11},{4,12},{5,13},{6,14},{7,15},{8,0},{9,1},... | collective-permute-start | bytes 1179656 | tf_op jit(solution)/shard_map/ppermute | solution.py:18
  256.6 143.8 %collective-permute-start.26 = (bf16[128,1536]{0,1:T(8,128)(2,1)S(1)}, bf16[128,1536]{0,1:T(8,128)(2,1)S(1)}, u32[]{:S(2)}, u32[]{:S(2)}) collective-permute-start(bf16[128,1536]{0,1:T(8,128)(2,1)S(1)} %copy.90), channel_id=1, source_target_pairs={{0,7},{1,8},{2,9},{3,10},{4,11},{5,12},{6,13},{7,14},{8,15},{9,0},... | collective-permute-start | bytes 1179656 | tf_op jit(solution)/shard_map/ppermute | solution.py:18
  262.1 141.4 %collective-permute-start.27 = (bf16[128,1536]{0,1:T(8,128)(2,1)S(1)}, bf16[128,1536]{0,1:T(8,128)(2,1)}, u32[]{:S(2)}, u32[]{:S(2)}) collective-permute-start(bf16[128,1536]{0,1:T(8,128)(2,1)S(1)} %copy.90), channel_id=1, source_target_pairs={{0,6},{1,7},{2,8},{3,9},{4,10},{5,11},{6,12},{7,13},{8,14},{9,15},... | collective-permute-start | bytes 1179656 | tf_op jit(solution)/shard_map/ppermute | solution.py:18
  264.7 141.0 %collective-permute-start.28 = (bf16[128,1536]{0,1:T(8,128)(2,1)S(1)}, bf16[128,1536]{0,1:T(8,128)(2,1)}, u32[]{:S(2)}, u32[]{:S(2)}) collective-permute-start(bf16[128,1536]{0,1:T(8,128)(2,1)S(1)} %copy.90), channel_id=1, source_target_pairs={{0,5},{1,6},{2,7},{3,8},{4,9},{5,10},{6,11},{7,12},{8,13},{9,14},{... | collective-permute-start | bytes 1179656 | tf_op jit(solution)/shard_map/ppermute | solution.py:18
  271.2 137.7 %collective-permute-start.29 = (bf16[128,1536]{0,1:T(8,128)(2,1)S(1)}, bf16[128,1536]{0,1:T(8,128)(2,1)}, u32[]{:S(2)}, u32[]{:S(2)}) collective-permute-start(bf16[128,1536]{0,1:T(8,128)(2,1)S(1)} %copy.90), channel_id=1, source_target_pairs={{0,3},{1,4},{2,5},{3,6},{4,7},{5,8},{6,9},{7,10},{8,11},{9,12},{10... | collective-permute-start | bytes 1179656 | tf_op jit(solution)/shard_map/ppermute | solution.py:18
  294.9 115.8 %collective-permute-start.30 = (bf16[128,1536]{0,1:T(8,128)(2,1)S(1)}, bf16[128,1536]{0,1:T(8,128)(2,1)}, u32[]{:S(2)}, u32[]{:S(2)}) collective-permute-start(bf16[128,1536]{0,1:T(8,128)(2,1)S(1)} %copy.90), channel_id=1, source_target_pairs={{0,2},{1,3},{2,4},{3,5},{4,6},{5,7},{6,8},{7,9},{8,10},{9,11},{10,... | collective-permute-start | bytes 1179656 | tf_op jit(solution)/shard_map/ppermute | solution.py:18
  424.4 55.3 %collective-permute-start.38 = (bf16[128,1536]{0,1:T(8,128)(2,1)S(1)}, bf16[128,1536]{0,1:T(8,128)(2,1)S(1)}, u32[]{:S(2)}, u32[]{:S(2)}) collective-permute-start(bf16[128,1536]{0,1:T(8,128)(2,1)S(1)} %copy.90), channel_id=1, source_target_pairs={{0,8},{1,9},{2,10},{3,11},{4,12},{5,13},{6,14},{7,15},{8,0},{9,1},... | collective-permute-start | bytes 1179656 | tf_op jit(solution)/shard_map/ppermute | solution.py:18
  435.2 83.9 %collective-permute-start.52 = (bf16[128,1536]{0,1:T(8,128)(2,1)S(1)}, bf16[128,1536]{0,1:T(8,128)(2,1)S(1)}, u32[]{:S(2)}, u32[]{:S(2)}) collective-permute-start(bf16[128,1536]{0,1:T(8,128)(2,1)S(1)} %bitcast.276), channel_id=1, source_target_pairs={{0,7},{1,8},{2,9},{3,10},{4,11},{5,12},{6,13},{7,14},{8,15},{9,0},... | collective-permute-start | bytes 1179656 | tf_op jit(solution)/shard_map/ppermute | solution.py:18
  438.2 87.0 %collective-permute-start.53 = (bf16[128,1536]{0,1:T(8,128)(2,1)S(1)}, bf16[128,1536]{0,1:T(8,128)(2,1)S(1)}, u32[]{:S(2)}, u32[]{:S(2)}) collective-permute-start(bf16[128,1536]{0,1:T(8,128)(2,1)S(1)} %bitcast.277), channel_id=1, source_target_pairs={{0,6},{1,7},{2,8},{3,9},{4,10},{5,11},{6,12},{7,13},{8,14},{9,15},... | collective-permute-start | bytes 1179656 | tf_op jit(solution)/shard_map/ppermute | solution.py:18
  444.1 82.4 %collective-permute-start.54 = (bf16[128,1536]{0,1:T(8,128)(2,1)S(1)}, bf16[128,1536]{0,1:T(8,128)(2,1)S(1)}, u32[]{:S(2)}, u32[]{:S(2)}) collective-permute-start(bf16[128,1536]{0,1:T(8,128)(2,1)S(1)} %bitcast.278), channel_id=1, source_target_pairs={{0,5},{1,6},{2,7},{3,8},{4,9},{5,10},{6,11},{7,12},{8,13},{9,14},{... | collective-permute-start | bytes 1179656 | tf_op jit(solution)/shard_map/ppermute | solution.py:18
  448.2 80.5 %collective-permute-start.55 = (bf16[128,1536]{0,1:T(8,128)(2,1)S(1)}, bf16[128,1536]{0,1:T(8,128)(2,1)S(1)}, u32[]{:S(2)}, u32[]{:S(2)}) collective-permute-start(bf16[128,1536]{0,1:T(8,128)(2,1)S(1)} %bitcast.279), channel_id=1, source_target_pairs={{0,3},{1,4},{2,5},{3,6},{4,7},{5,8},{6,9},{7,10},{8,11},{9,12},{10... | collective-permute-start | bytes 1179656 | tf_op jit(solution)/shard_map/ppermute | solution.py:18
  479.7 50.8 %collective-permute-start.56 = (bf16[128,1536]{0,1:T(8,128)(2,1)S(1)}, bf16[128,1536]{0,1:T(8,128)(2,1)S(1)}, u32[]{:S(2)}, u32[]{:S(2)}) collective-permute-start(bf16[128,1536]{0,1:T(8,128)(2,1)S(1)} %bitcast.280), channel_id=1, source_target_pairs={{0,2},{1,3},{2,4},{3,5},{4,6},{5,7},{6,8},{7,9},{8,10},{9,11},{10,... | collective-permute-start | bytes 1179656 | tf_op jit(solution)/shard_map/ppermute | solution.py:18
  561.0 41.2 %collective-permute-start.64 = (bf16[128,1536]{0,1:T(8,128)(2,1)S(1)}, bf16[128,1536]{0,1:T(8,128)(2,1)S(1)}, u32[]{:S(2)}, u32[]{:S(2)}) collective-permute-start(bf16[128,1536]{0,1:T(8,128)(2,1)S(1)} %bitcast.288), channel_id=1, source_target_pairs={{0,8},{1,9},{2,10},{3,11},{4,12},{5,13},{6,14},{7,15},{8,0},{9,1},... | collective-permute-start | bytes 1179656 | tf_op jit(solution)/shard_map/ppermute | solution.py:18
  561.8 51.9 %collective-permute-start.39 = (f32[128,12]{0,1:T(8,128)S(1)}, f32[128,12]{0,1:T(8,128)S(1)}, u32[]{:S(2)}, u32[]{:S(2)}) collective-permute-start(f32[128,12]{0,1:T(8,128)S(1)} %bitcast.296), channel_id=1, source_target_pairs={{0,7},{1,8},{2,9},{3,10},{4,11},{5,12},{6,13},{7,14},{8,15},{9,0},... | collective-permute-start | bytes 18440 | tf_op jit(solution)/shard_map/ppermute | solution.py:18
  564.3 57.2 %collective-permute-start.40 = (f32[128,12]{0,1:T(8,128)S(1)}, f32[128,12]{0,1:T(8,128)S(1)}, u32[]{:S(2)}, u32[]{:S(2)}) collective-permute-start(f32[128,12]{0,1:T(8,128)S(1)} %bitcast.297), channel_id=1, source_target_pairs={{0,6},{1,7},{2,8},{3,9},{4,10},{5,11},{6,12},{7,13},{8,14},{9,15},... | collective-permute-start | bytes 18440 | tf_op jit(solution)/shard_map/ppermute | solution.py:18
  572.5 49.1 %collective-permute-start.41 = (f32[128,12]{0,1:T(8,128)S(1)}, f32[128,12]{0,1:T(8,128)S(1)}, u32[]{:S(2)}, u32[]{:S(2)}) collective-permute-start(f32[128,12]{0,1:T(8,128)S(1)} %bitcast.298), channel_id=1, source_target_pairs={{0,5},{1,6},{2,7},{3,8},{4,9},{5,10},{6,11},{7,12},{8,13},{9,14},{... | collective-permute-start | bytes 18440 | tf_op jit(solution)/shard_map/ppermute | solution.py:18
  577.2 44.4 %collective-permute-start.42 = (f32[128,12]{0,1:T(8,128)S(1)}, f32[128,12]{0,1:T(8,128)S(1)}, u32[]{:S(2)}, u32[]{:S(2)}) collective-permute-start(f32[128,12]{0,1:T(8,128)S(1)} %bitcast.299), channel_id=1, source_target_pairs={{0,3},{1,4},{2,5},{3,6},{4,7},{5,8},{6,9},{7,10},{8,11},{9,12},{10... | collective-permute-start | bytes 18440 | tf_op jit(solution)/shard_map/ppermute | solution.py:18
  (61 other events, 1132.4 us)
where the time goes:
time: 705 us; the launch traced here: 701 us
  starting transfers between devices  381 us (54%)
  waiting for transfers between devices  138 us (20%)
  local copies, waits for them, and re-layouts  81 us (11%)
  matrix products  76.5 us (11%)
  loops' own time  17.8 us (3%)
    ppermute x78, starting transfers between devices, from_behind(): lax.ppermute(value, axis, [(i, (i + by) % count) for i in range(count)])  381 us
    ppermute x78, waiting for transfers between devices, from_behind(): lax.ppermute(value, axis, [(i, (i + by) % count) for i in range(count)])  138 us
    unnamed x91, local copies, waits for them, and re-layouts  55.4 us
    dot_general x3, matrix products, query_group(): jnp.einsum('hqk,khd->qhd', grad_scores, key_part, preferred_element_type=...  14.8 us
  transfers between devices with their start and end apart: 78, of which 18 were waited for; matrix products, arithmetic and copies ran while one was open for 17% of the time, Pallas kernels for 0%

commit v1 on v0

--- a/solution.py
+++ b/solution.py
@@ -1,6 +1,10 @@
+import functools
+
 import jax
 import jax.numpy as jnp
 from jax import lax
+from jax.experimental import pallas as pl
+from jax.experimental.pallas import tpu as pltpu
 from jax.sharding import PartitionSpec as P
 
 HEADS = 12
@@ -11,6 +15,7 @@
 
 head_batch = 4
 masked_score = -1e30
+VMEM_BYTES = 48 * 1024 * 1024
 
 
 def from_behind(value, axis, by):
@@ -217,23 +222,300 @@
     return (out, grad_query, grad_key, grad_value)
 
 
+def head_owner(head, devices):
+    chips = devices // 2
+    first = (chips - (HEADS - chips)) // 2
+    return jnp.where(head < chips, 2 * head, 2 * (head - chips + first) + 1)
+
+
+def head_of(device, devices):
+    chips = devices // 2
+    extra = HEADS - chips
+    first = (chips - extra) // 2
+    chip = device // 2
+    odd = device % 2
+    inside = (chip >= first) & (chip < first + extra)
+    second = jnp.where(inside, chips + chip - first, -1)
+    return jnp.where(odd == 0, jnp.where(chip < HEADS, chip, -1), second)
+
+
+def exchange_kernel(
+    devices,
+    query_ref,
+    key_ref,
+    value_ref,
+    grad_ref,
+    slots_ref,
+    out_ref,
+    dq_ref,
+    dk_ref,
+    dv_ref,
+    q_all,
+    k_all,
+    v_all,
+    g_all,
+    kt_all,
+    vt_all,
+    gt_all,
+    ot_all,
+    o_all,
+    dq_all,
+    dk_all,
+    dv_all,
+    dk_sum,
+    dv_sum,
+    bias,
+    probs,
+    in_send,
+    in_recv,
+    out_send,
+    out_recv,
+):
+    me = lax.axis_index("ctx")
+    my_head = head_of(me, devices)
+    owns = my_head >= 0
+    tokens = devices * BLOCK
+    width = devices // (2 * TILE_H)
+    row_tokens = width * BLOCK
+    plane_tokens = tokens // 2
+    scaling = HEAD ** (-0.5)
+
+    barrier = pltpu.get_barrier_semaphore()
+    for step in range(1, devices):
+        pl.semaphore_signal(
+            barrier,
+            inc=1,
+            device_id={"ctx": lax.rem(me + step, devices)},
+            device_id_type=pl.DeviceIdType.MESH,
+        )
+    pl.semaphore_wait(barrier, devices - 1)
+
+    sources = (key_ref, query_ref, value_ref, grad_ref)
+    landings = (k_all, q_all, v_all, g_all)
+    own_rows = pl.ds(pl.multiple_of(me * BLOCK, BLOCK), BLOCK)
+
+    def send_inputs(index):
+        source, landing = sources[index], landings[index]
+
+        def one(step, carry):
+            head = lax.rem(me + step, HEADS)
+            owner = head_owner(head, devices)
+            columns = pl.ds(pl.multiple_of(head * HEAD, HEAD), HEAD)
+
+            @pl.when(owner != me)
+            def _():
+                pltpu.make_async_remote_copy(
+                    src_ref=source.at[:, columns],
+                    dst_ref=landing.at[own_rows, :],
+                    send_sem=in_send.at[index],
+                    recv_sem=in_recv.at[index],
+                    device_id={"ctx": owner},
+                    device_id_type=pl.DeviceIdType.MESH,
+                ).start()
+
+            @pl.when(owner == me)
+            def _():
+                pltpu.make_async_copy(
+                    source.at[:, columns], landing.at[own_rows, :], in_recv.at[index]
+                ).start()
+
+            return carry
+
+        lax.fori_loop(0, HEADS, one, 0)
+
+    for index in range(4):
+        send_inputs(index)
+
+    def arrived(index):
+        pltpu.make_async_copy(landings[index], landings[index], in_recv.at[index]).wait()
+
+    results = (o_all, dq_all, dk_all, dv_all)
+    targets = (out_ref, dq_ref, dk_ref, dv_ref)
+
+    def send_results(index):
+        result, target = results[index], targets[index]
+        columns = pl.ds(pl.multiple_of(my_head * HEAD, HEAD), HEAD)
+
+        def one(step, carry):
+            other = lax.rem(me + step, devices)
+            rows = pl.ds(pl.multiple_of(other * BLOCK, BLOCK), BLOCK)
+            pltpu.make_async_remote_copy(
+                src_ref=result.at[rows, :],
+                dst_ref=target.at[:, columns],
+                send_sem=out_send.at[index],
+                recv_sem=out_recv.at[index],
+                device_id={"ctx": other},
+                device_id_type=pl.DeviceIdType.MESH,
+            ).start()
+            return carry
+
+        lax.fori_loop(1, devices, one, 0)
+        pltpu.make_async_copy(
+            result.at[own_rows, :], target.at[:, columns], out_recv.at[index]
+        ).start()
+
+    def dot(left, right):
+        return jnp.dot(left, right, preferred_element_type=jnp.float32)
+
+    def dot_nt(left, right):
+        return lax.dot_general(
+            left, right, (((1,), (1,)), ((), ())), preferred_element_type=jnp.float32
+        )
+
+    def flip(ref, target):
+        for start in range(0, tokens, row_tokens):
+            part = ref[start : start + row_tokens, :].astype(jnp.float32)
+            target[:, start : start + row_tokens] = jnp.transpose(part).astype(target.dtype)
+
+    groups = []
+    for row in range(TILE_H):
+        low, high = max(row - 1, 0), min(row + 1, TILE_H - 1)
+        count = (high + 1 - low) * row_tokens
+        for plane in range(2):
+            groups.append(
+                (
+                    plane * plane_tokens + row * row_tokens,
+                    [(0, low * row_tokens), (count, plane_tokens + low * row_tokens)],
+                    count,
+                )
+            )
+
+    @pl.when(owns)
+    def _():
+        for block in range(devices):
+            listed = slots_ref[block : block + 1, :]
+            ids = lax.broadcasted_iota(jnp.int32, (devices, listed.shape[1]), 0)
+            hit = jnp.where(ids == listed, 0.0, -1e30)
+            best = jnp.max(hit, axis=1, keepdims=True)
+            bias[:, block * BLOCK : (block + 1) * BLOCK] = jnp.broadcast_to(best, (devices, BLOCK))
+        dk_sum[...] = jnp.zeros_like(dk_sum)
+        dv_sum[...] = jnp.zeros_like(dv_sum)
+
+        arrived(0)
+        arrived(1)
+        flip(k_all, kt_all)
+        for index, (start, ranges, count) in enumerate(groups):
+            queries = q_all[start : start + row_tokens, :]
+            scores = []
+            for offset, first in ranges:
+                part = dot_nt(k_all[first : first + count, :], queries) * scaling
+                blocks = count // BLOCK
+                shift = bias[first // BLOCK : first // BLOCK + blocks, start : start + row_tokens]
+                part = part.reshape(blocks, BLOCK, row_tokens) + shift[:, None, :]
+                scores.append(part.reshape(count, row_tokens))
+            peak = jnp.maximum(
+                jnp.max(scores[0], axis=0, keepdims=True), jnp.max(scores[1], axis=0, keepdims=True)
+            )
+            powers = [jnp.exp(part - peak) for part in scores]
+            total = jnp.sum(powers[0], axis=0, keepdims=True) + jnp.sum(
+                powers[1], axis=0, keepdims=True
+            )
+            inverse = 1.0 / total
+            for (offset, first), part in zip(ranges, powers):
+                probs[index, offset : offset + count, :] = part * inverse
+
+        arrived(2)
+        flip(v_all, vt_all)
+        for index, (start, ranges, count) in enumerate(groups):
+            mixed = jnp.zeros((HEAD, row_tokens), jnp.float32)
+            for offset, first in ranges:
+                weights = probs[index, offset : offset + count, :].astype(jnp.bfloat16)
+                mixed += dot(vt_all[:, first : first + count], weights)
+            ot_all[:, start : start + row_tokens] = mixed.astype(jnp.bfloat16)
+            o_all[start : start + row_tokens, :] = jnp.transpose(mixed).astype(jnp.bfloat16)
+        send_results(0)
+
+        arrived(3)
+        flip(g_all, gt_all)
+        for index, (start, ranges, count) in enumerate(groups):
+            span = slice(start, start + row_tokens)
+            delta = jnp.sum(
+                gt_all[:, span].astype(jnp.float32) * ot_all[:, span].astype(jnp.float32),
+                axis=0,
+                keepdims=True,
+            )
+            grads = g_all[span, :]
+            queries = q_all[span, :]
+            turned = jnp.zeros((HEAD, row_tokens), jnp.float32)
+            for offset, first in ranges:
+                keys = slice(first, first + count)
+                exact = probs[index, offset : offset + count, :]
+                dv_sum[keys, :] += dot(exact.astype(jnp.bfloat16), grads)
+                product = dot_nt(v_all[keys, :], grads)
+                slopes = (exact * (product - delta)).astype(jnp.bfloat16)
+                turned += dot(kt_all[:, keys], slopes)
+                dk_sum[keys, :] += dot(slopes, queries)
+            dq_all[span, :] = jnp.transpose(turned * scaling).astype(jnp.bfloat16)
+        dv_all[...] = dv_sum[...].astype(jnp.bfloat16)
+        send_results(3)
+        dk_all[...] = (dk_sum[...] * scaling).astype(jnp.bfloat16)
+        send_results(2)
+        send_results(1)
+
+        for index in range(4):
+            sent = sources[index].at[:, : (HEADS - 1) * HEAD]
+            pltpu.make_async_copy(sent, sent, in_send.at[index]).wait()
+            sent = results[index].at[: (devices - 1) * BLOCK, :]
+            pltpu.make_async_copy(sent, sent, out_send.at[index]).wait()
+
+    @pl.when(jnp.logical_not(owns))
+    def _():
+        for index in range(4):
+            pltpu.make_async_copy(sources[index], sources[index], in_send.at[index]).wait()
+
+    for index in range(4):
+        pltpu.make_async_copy(targets[index], targets[index], out_recv.at[index]).wait()
+
+
+def exchange_sizes(devices):
+    tokens = devices * BLOCK
+    row_tokens = tokens // (2 * TILE_H)
+    return tokens, (2 * TILE_H, 6 * row_tokens, row_tokens)
+
+
+def exchange_body(query, key_rows, value, grad_out, kv_slots):
+    devices = lax.axis_size("ctx")
+    tokens, probs_shape = exchange_sizes(devices)
+    low = lambda *shape: pltpu.VMEM(shape, jnp.bfloat16)
+    full = lambda *shape: pltpu.VMEM(shape, jnp.float32)
+    anywhere = pl.BlockSpec(memory_space=pl.ANY)
+    whole = jax.ShapeDtypeStruct(query.shape, query.dtype)
+    return pl.pallas_call(
+        functools.partial(exchange_kernel, devices),
+        out_shape=(whole,) * 4,
+        in_specs=[anywhere] * 4 + [pl.BlockSpec(memory_space=pltpu.VMEM)],
+        out_specs=(anywhere,) * 4,
+        scratch_shapes=[low(tokens, HEAD)] * 4
+        + [low(HEAD, tokens)] * 4
+        + [low(tokens, HEAD)] * 4
+        + [full(tokens, HEAD)] * 2
+        + [full(devices, tokens), full(*probs_shape)]
+        + [pltpu.SemaphoreType.DMA((4,))] * 4,
+        compiler_params=pltpu.CompilerParams(
+            collective_id=0, has_side_effects=True, vmem_limit_bytes=VMEM_BYTES
+        ),
+    )(query, key_rows, value, grad_out, kv_slots)
+
+
+def fits_exchange(devices, rows):
+    if rows != devices * BLOCK or devices % (2 * TILE_H) or not devices // 2 <= HEADS <= devices:
+        return False
+    _, (groups, keys, queries) = exchange_sizes(devices)
+    return groups * keys * queries * 4 <= VMEM_BYTES // 2
+
+
 def solution(mesh):
-    placed = (
-        P(("groups", "ctx"), None),
-        P(("groups", "ctx"), None),
-        P(("groups", "ctx"), None),
-        P(("groups", "ctx"), None),
-        P(),
-    )
-    return jax.shard_map(
-        body,
-        mesh=mesh,
-        in_specs=placed,
-        out_specs=(
-            P(("groups", "ctx"), None),
-            P(("groups", "ctx"), None),
-            P(("groups", "ctx"), None),
-            P(("groups", "ctx"), None),
-        ),
-        check_vma=False,
-    )
+    placed = P(("groups", "ctx"), None)
+
+    def chosen(query, key_rows, value, grad_out, kv_slots):
+        devices = mesh.shape["ctx"]
+        rows = query.shape[0] // mesh.shape["groups"]
+        return jax.shard_map(
+            exchange_body if fits_exchange(devices, rows) else body,
+            mesh=mesh,
+            in_specs=(placed,) * 4 + (P(),),
+            out_specs=(placed,) * 4,
+            check_vma=False,
+        )(query, key_rows, value, grad_out, kv_slots)
+
+    return chosen

time: 705 us -> 82 us (0.12)
  starting transfers between devices: 381 us -> 0 us
  waiting for transfers between devices: 138 us -> 0 us
  matrix products: 76.5 us -> 0 us
  Pallas kernels: 0 us -> 73.4 us
  local copies, waits for them, and re-layouts: 81 us -> 7.66 us
  loops' own time: 17.8 us -> 0 us
    ppermute x78 -> x0, starting transfers between devices: 381 us -> none  [from_behind(): lax.ppermute(value, axis, [(i, (i + by) % count) for i in range(count)])]
    ppermute x78 -> x0, waiting for transfers between devices: 138 us -> none  [from_behind(): lax.ppermute(value, axis, [(i, (i + by) % count) for i in range(count)])]
    dot_general x21 -> x0, matrix products: 76.5 us -> none  [the longest x3 14.8 us: query_group(): jnp.einsum('hqk,khd->qhd', grad_scores, key_part, preferred_element_type=...]
    pallas_call x0 -> x1, Pallas kernels: none -> 73.4 us  [exchange_body(): pl.pallas_call(functools.partial(exchange_kernel, devices), out_shape=(wh...]
    unnamed x91 -> x14, local copies, waits for them, and re-layouts: 55.4 us -> 7.66 us
    another operation x3 -> x0, loops' own time: 17.8 us -> none  [the longest x1 5.95 us: body(): lax.map(lambda group_index: key_group(group_index, own_keys, own_values,...]
    while x8 -> x0, local copies, waits for them, and re-layouts: 8.51 us -> none  [the longest x2 8.5 us: body(): lax.map(lambda group_index: forward_group(group_index, queries, cand_keys...]
  transfers between devices with their start and end apart: 78 -> 0, of which waited for: 18 -> 0; matrix products, arithmetic and copies ran while one was open for 17% -> 0% of each run, Pallas kernels for 0% -> 0%
where the time goes in v1:
time: 82 us; the launch traced here: 81.7 us
  Pallas kernels  73.4 us (90%)
  local copies, waits for them, and re-layouts  7.66 us (9%)
    pallas_call x1, Pallas kernels, exchange_body(): pl.pallas_call(functools.partial(exchange_kernel, devices), out_shape=(wh...  73.4 us
    unnamed x14, local copies, waits for them, and re-layouts  7.66 us

profile of v1, /device:TPU:15, one launch (start us, length us, event | category | flops | bytes accessed | tf_op | source)
XLA Modules:
  0.0 81.7 jit_solution(8602777246393457676)
XLA Ops:
  0.6 0.0 copy-start
  0.6 1.0 %copy-done = bf16[128,1536]{1,0:T(8,128)(2,1)S(1)} copy-done((bf16[128,1536]{1,0:T(8,128)(2,1)S(1)}, bf16[128,1536]{1,0:T(8,128)(2,1)}, u32[]{:S(2)}) %copy-start) | copy-done | bytes 393240
  1.6 0.0 copy-start.1
  1.6 1.0 %copy-done.1 = bf16[128,1536]{1,0:T(8,128)(2,1)S(1)} copy-done((bf16[128,1536]{1,0:T(8,128)(2,1)S(1)}, bf16[128,1536]{1,0:T(8,128)(2,1)}, u32[]{:S(2)}) %copy-start.1) | copy-done | bytes 393240
  2.6 0.0 copy-start.2
  2.6 1.0 %copy-done.2 = bf16[128,1536]{1,0:T(8,128)(2,1)S(1)} copy-done((bf16[128,1536]{1,0:T(8,128)(2,1)S(1)}, bf16[128,1536]{1,0:T(8,128)(2,1)}, u32[]{:S(2)}) %copy-start.2) | copy-done | bytes 393240
  3.6 0.0 copy-start.3
  3.6 1.0 %copy-done.3 = bf16[128,1536]{1,0:T(8,128)(2,1)S(1)} copy-done((bf16[128,1536]{1,0:T(8,128)(2,1)S(1)}, bf16[128,1536]{1,0:T(8,128)(2,1)}, u32[]{:S(2)}) %copy-start.3) | copy-done | bytes 393240
  4.6 0.0 copy-start.4
  4.6 0.7 copy-done.4
  5.3 73.4 %shard_map.84 = (bf16[128,1536]{1,0:T(8,128)(2,1)S(1)}, bf16[128,1536]{1,0:T(8,128)(2,1)S(1)}, bf16[128,1536]{1,0:T(8,128)(2,1)S(1)}, bf16[128,1536]{1,0:T(8,128)(2,1)S(1)}) custom-call(bf16[128,1536]{1,0:T(8,128)(2,1)S(1)} %copy-done, bf16[128,1536]{1,0:T(8,128)(2,1)S(1)} %copy-done.1, bf16[128,1536]{1,0:T(8,128)(2,1)S(1)} %copy-done.2, ...), custom_call_target="tpu_custom_call" | custom-call | tf_op jit(solution)/shard_map/pallas_call | solution.py:483
  78.7 0.7 copy.13
  79.4 0.7 copy.14
  80.2 0.7 copy.15
  80.9 0.7 copy.16
Async XLA Ops:
  0.6 1.0 %copy-start = (bf16[128,1536]{1,0:T(8,128)(2,1)S(1)}, bf16[128,1536]{1,0:T(8,128)(2,1)}, u32[]{:S(2)}) copy-start(bf16[128,1536]{1,0:T(8,128)(2,1)} %query_ref.1) | copy-start | bytes 1179652
  1.6 1.0 %copy-start.1 = (bf16[128,1536]{1,0:T(8,128)(2,1)S(1)}, bf16[128,1536]{1,0:T(8,128)(2,1)}, u32[]{:S(2)}) copy-start(bf16[128,1536]{1,0:T(8,128)(2,1)} %key_ref.1) | copy-start | bytes 1179652
  2.6 1.0 %copy-start.2 = (bf16[128,1536]{1,0:T(8,128)(2,1)S(1)}, bf16[128,1536]{1,0:T(8,128)(2,1)}, u32[]{:S(2)}) copy-start(bf16[128,1536]{1,0:T(8,128)(2,1)} %value_ref.1) | copy-start | bytes 1179652
  3.6 1.0 %copy-start.3 = (bf16[128,1536]{1,0:T(8,128)(2,1)S(1)}, bf16[128,1536]{1,0:T(8,128)(2,1)}, u32[]{:S(2)}) copy-start(bf16[128,1536]{1,0:T(8,128)(2,1)} %grad_ref.1) | copy-start | bytes 1179652
  4.6 0.7 copy-start.4

commit v2 on v1

--- a/solution.py
+++ b/solution.py
@@ -15,7 +15,7 @@
 
 head_batch = 4
 masked_score = -1e30
-VMEM_BYTES = 48 * 1024 * 1024
+VMEM_BYTES = 63 * 1024 * 1024
 
 
 def from_behind(value, axis, by):
@@ -294,34 +294,44 @@
     landings = (k_all, q_all, v_all, g_all)
     own_rows = pl.ds(pl.multiple_of(me * BLOCK, BLOCK), BLOCK)
 
+    half = me // (devices // 2)
+    chips = devices // 2
+    pairs = HEADS // 2
+
     def send_inputs(index):
         source, landing = sources[index], landings[index]
 
         def one(step, carry):
-            head = lax.rem(me + step, HEADS)
-            owner = head_owner(head, devices)
-            columns = pl.ds(pl.multiple_of(head * HEAD, HEAD), HEAD)
-
-            @pl.when(owner != me)
-            def _():
-                pltpu.make_async_remote_copy(
-                    src_ref=source.at[:, columns],
-                    dst_ref=landing.at[own_rows, :],
-                    send_sem=in_send.at[index],
-                    recv_sem=in_recv.at[index],
-                    device_id={"ctx": owner},
-                    device_id_type=pl.DeviceIdType.MESH,
-                ).start()
-
-            @pl.when(owner == me)
-            def _():
-                pltpu.make_async_copy(
-                    source.at[:, columns], landing.at[own_rows, :], in_recv.at[index]
-                ).start()
+            place = lax.rem(me + step, pairs)
+            for side in (1 - half, half):
+                head = jnp.where(
+                    place < chips // 2,
+                    place + side * (chips // 2),
+                    chips + place - chips // 2 + side * ((HEADS - chips) // 2),
+                )
+                owner = head_owner(head, devices)
+                columns = pl.ds(pl.multiple_of(head * HEAD, HEAD), HEAD)
+
+                @pl.when(owner != me)
+                def _():
+                    pltpu.make_async_remote_copy(
+                        src_ref=source.at[:, columns],
+                        dst_ref=landing.at[own_rows, :],
+                        send_sem=in_send.at[index],
+                        recv_sem=in_recv.at[index],
+                        device_id={"ctx": owner},
+                        device_id_type=pl.DeviceIdType.MESH,
+                    ).start()
+
+                @pl.when(owner == me)
+                def _():
+                    pltpu.make_async_copy(
+                        source.at[:, columns], landing.at[own_rows, :], in_recv.at[index]
+                    ).start()
 
             return carry
 
-        lax.fori_loop(0, HEADS, one, 0)
+        lax.fori_loop(0, pairs, one, 0)
 
     for index in range(4):
         send_inputs(index)
@@ -332,27 +342,30 @@
     results = (o_all, dq_all, dk_all, dv_all)
     targets = (out_ref, dq_ref, dk_ref, dv_ref)
 
-    def send_results(index):
+    def send_row(index, row):
         result, target = results[index], targets[index]
         columns = pl.ds(pl.multiple_of(my_head * HEAD, HEAD), HEAD)
-
-        def one(step, carry):
-            other = lax.rem(me + step, devices)
-            rows = pl.ds(pl.multiple_of(other * BLOCK, BLOCK), BLOCK)
-            pltpu.make_async_remote_copy(
-                src_ref=result.at[rows, :],
-                dst_ref=target.at[:, columns],
-                send_sem=out_send.at[index],
-                recv_sem=out_recv.at[index],
-                device_id={"ctx": other},
-                device_id_type=pl.DeviceIdType.MESH,
-            ).start()
-            return carry
-
-        lax.fori_loop(1, devices, one, 0)
-        pltpu.make_async_copy(
-            result.at[own_rows, :], target.at[:, columns], out_recv.at[index]
-        ).start()
+        for column in range(width):
+            for side in (1 - half, half):
+                other = side * (devices // 2) + row * width + column
+                rows = pl.ds(pl.multiple_of(other * BLOCK, BLOCK), BLOCK)
+
+                @pl.when(other != me)
+                def _():
+                    pltpu.make_async_remote_copy(
+                        src_ref=result.at[rows, :],
+                        dst_ref=target.at[:, columns],
+                        send_sem=out_send.at[index],
+                        recv_sem=out_recv.at[index],
+                        device_id={"ctx": other},
+                        device_id_type=pl.DeviceIdType.MESH,
+                    ).start()
+
+                @pl.when(other == me)
+                def _():
+                    pltpu.make_async_copy(
+                        result.at[rows, :], target.at[:, columns], out_recv.at[index]
+                    ).start()
 
     def dot(left, right):
         return jnp.dot(left, right, preferred_element_type=jnp.float32)
@@ -379,6 +392,15 @@
                     count,
                 )
             )
+
+    def finish_keys(row):
+        for plane in range(2):
+            start = plane * plane_tokens + row * row_tokens
+            span = slice(start, start + row_tokens)
+            dv_all[span, :] = dv_sum[span, :].astype(jnp.bfloat16)
+            dk_all[span, :] = (dk_sum[span, :] * scaling).astype(jnp.bfloat16)
+        send_row(3, row)
+        send_row(2, row)
 
     @pl.when(owns)
     def _():
@@ -423,7 +445,8 @@
                 mixed += dot(vt_all[:, first : first + count], weights)
             ot_all[:, start : start + row_tokens] = mixed.astype(jnp.bfloat16)
             o_all[start : start + row_tokens, :] = jnp.transpose(mixed).astype(jnp.bfloat16)
-        send_results(0)
+            if index % 2 == 1:
+                send_row(0, index // 2)
 
         arrived(3)
         flip(g_all, gt_all)
@@ -446,11 +469,12 @@
                 turned += dot(kt_all[:, keys], slopes)
                 dk_sum[keys, :] += dot(slopes, queries)
             dq_all[span, :] = jnp.transpose(turned * scaling).astype(jnp.bfloat16)
-        dv_all[...] = dv_sum[...].astype(jnp.bfloat16)
-        send_results(3)
-        dk_all[...] = (dk_sum[...] * scaling).astype(jnp.bfloat16)
-        send_results(2)
-        send_results(1)
+            if index % 2 == 1:
+                row = index // 2
+                send_row(1, row)
+                if row >= 1:
+                    finish_keys(row - 1)
+        finish_keys(TILE_H - 1)
 
         for index in range(4):
             sent = sources[index].at[:, : (HEADS - 1) * HEAD]

time: 82 us -> 79.5 us (0.970)
  local copies, waits for them, and re-layouts: 7.66 us -> 4.84 us
    unnamed x14 -> x10, local copies, waits for them, and re-layouts: 7.66 us -> 4.84 us
where the time goes in v2:
time: 79.5 us; the launch traced here: 79.3 us
  Pallas kernels  73.8 us (93%)
  local copies, waits for them, and re-layouts  4.84 us (6%)
    pallas_call x1, Pallas kernels, exchange_body(): pl.pallas_call(functools.partial(exchange_kernel, devices), out_shape=(wh...  73.8 us
    unnamed x10, local copies, waits for them, and re-layouts  4.84 us

profile of v2, /device:TPU:15, one launch (start us, length us, event | category | flops | bytes accessed | tf_op | source)
XLA Modules:
  0.0 79.3 jit_solution(10517285974085205656)
XLA Ops:
  0.6 73.8 %shard_map.84 = (bf16[128,1536]{1,0:T(8,128)(2,1)}, bf16[128,1536]{1,0:T(8,128)(2,1)}, bf16[128,1536]{1,0:T(8,128)(2,1)}, bf16[128,1536]{1,0:T(8,128)(2,1)}) custom-call(bf16[128,1536]{1,0:T(8,128)(2,1)} %query_ref.1, bf16[128,1536]{1,0:T(8,128)(2,1)} %key_ref.1, bf16[128,1536]{1,0:T(8,128)(2,1)} %value_ref.1, bf16[128,1536]{1,0:T(8,128)(2,1)} %grad_ref.1, ...), custom_call_target="tpu_custom_call" | custom-call | tf_op jit(solution)/shard_map/pallas_call | solution.py:507
  74.4 0.0 copy-start.2
  74.4 1.8 %copy.13 = bf16[128,1536]{1,0:T(8,128)(2,1)} copy(bf16[128,1536]{1,0:T(8,128)(2,1)} %get-tuple-element.8) | data formatting | bytes 786432
  76.2 0.0 copy-done.2
  76.2 0.0 copy-start.1
  76.2 0.7 copy.14
  77.0 0.4 copy-done.1
  77.4 0.0 copy-start
  77.4 0.7 copy.15
  78.1 0.4 copy-done
  78.5 0.7 copy.16
Async XLA Ops:
  74.4 1.8 %copy-start.2 = (bf16[128,1536]{1,0:T(8,128)(2,1)S(1)}, bf16[128,1536]{1,0:T(8,128)(2,1)}, u32[]{:S(2)}) copy-start(bf16[128,1536]{1,0:T(8,128)(2,1)} %get-tuple-element.9) | copy-start | bytes 1179652
  76.2 1.1 %copy-start.1 = (bf16[128,1536]{1,0:T(8,128)(2,1)S(1)}, bf16[128,1536]{1,0:T(8,128)(2,1)}, u32[]{:S(2)}) copy-start(bf16[128,1536]{1,0:T(8,128)(2,1)} %get-tuple-element.10) | copy-start | bytes 1179652
  77.4 1.1 %copy-start = (bf16[128,1536]{1,0:T(8,128)(2,1)S(1)}, bf16[128,1536]{1,0:T(8,128)(2,1)}, u32[]{:S(2)}) copy-start(bf16[128,1536]{1,0:T(8,128)(2,1)} %get-tuple-element.11) | copy-start | bytes 1179652

commit v3 on v2

--- a/solution.py
+++ b/solution.py
@@ -333,8 +333,22 @@
 
         lax.fori_loop(0, pairs, one, 0)
 
-    for index in range(4):
-        send_inputs(index)
+    def inputs_sent(index):
+        @pl.when(owns)
+        def _():
+            sent = sources[index].at[:, : (HEADS - 1) * HEAD]
+            pltpu.make_async_copy(sent, sent, in_send.at[index]).wait()
+
+        @pl.when(jnp.logical_not(owns))
+        def _():
+            pltpu.make_async_copy(sources[index], sources[index], in_send.at[index]).wait()
+
+    send_inputs(0)
+    send_inputs(1)
+    inputs_sent(0)
+    send_inputs(2)
+    inputs_sent(1)
+    send_inputs(3)
 
     def arrived(index):
         pltpu.make_async_copy(landings[index], landings[index], in_recv.at[index]).wait()
@@ -477,18 +491,25 @@
         finish_keys(TILE_H - 1)
 
         for index in range(4):
-            sent = sources[index].at[:, : (HEADS - 1) * HEAD]
-            pltpu.make_async_copy(sent, sent, in_send.at[index]).wait()
             sent = results[index].at[: (devices - 1) * BLOCK, :]
             pltpu.make_async_copy(sent, sent, out_send.at[index]).wait()
 
-    @pl.when(jnp.logical_not(owns))
-    def _():
-        for index in range(4):
-            pltpu.make_async_copy(sources[index], sources[index], in_send.at[index]).wait()
-
+    inputs_sent(2)
+    inputs_sent(3)
     for index in range(4):
         pltpu.make_async_copy(targets[index], targets[index], out_recv.at[index]).wait()
+
+
+def copy_kernel(*refs):
+    sources, targets, sems = refs[:4], refs[4:8], refs[8]
+    copies = [
+        pltpu.make_async_copy(source, target, sems.at[index])
+        for index, (source, target) in enumerate(zip(sources, targets))
+    ]
+    for copy in copies:
+        copy.start()
+    for copy in copies:
+        copy.wait()
 
 
 def exchange_sizes(devices):
@@ -504,7 +525,7 @@
     full = lambda *shape: pltpu.VMEM(shape, jnp.float32)
     anywhere = pl.BlockSpec(memory_space=pl.ANY)
     whole = jax.ShapeDtypeStruct(query.shape, query.dtype)
-    return pl.pallas_call(
+    landed = pl.pallas_call(
         functools.partial(exchange_kernel, devices),
         out_shape=(whole,) * 4,
         in_specs=[anywhere] * 4 + [pl.BlockSpec(memory_space=pltpu.VMEM)],
@@ -519,6 +540,14 @@
             collective_id=0, has_side_effects=True, vmem_limit_bytes=VMEM_BYTES
         ),
     )(query, key_rows, value, grad_out, kv_slots)
+    return pl.pallas_call(
+        copy_kernel,
+        out_shape=(whole,) * 4,
+        in_specs=[anywhere] * 4,
+        out_specs=(anywhere,) * 4,
+        scratch_shapes=[pltpu.SemaphoreType.DMA((4,))],
+        compiler_params=pltpu.CompilerParams(vmem_limit_bytes=VMEM_BYTES),
+    )(*landed)
 
 
 def fits_exchange(devices, rows):

time: 79.5 us -> 123 us (1.55)
  Pallas kernels: 73.8 us -> 123 us
  local copies, waits for them, and re-layouts: 4.84 us -> 0 us
    pallas_call x0 -> x1, Pallas kernels: none -> 48.8 us  [exchange_body(): pl.pallas_call(copy_kernel, out_shape=(whole,) * 4, in_specs=[anywhere] *...]
    unnamed x10 -> x0, local copies, waits for them, and re-layouts: 4.84 us -> none
where the time goes in v3:
time: 123 us
  Pallas kernels  123 us (100%)
    pallas_call x1, Pallas kernels, exchange_body(): pl.pallas_call(functools.partial(exchange_kernel, devices), out_shape=(wh...  73.8 us
    pallas_call x1, Pallas kernels, exchange_body(): pl.pallas_call(copy_kernel, out_shape=(whole,) * 4, in_specs=[anywhere] *...  48.8 us

profile of v3, /device:TPU:15, one launch (start us, length us, event | category | flops | bytes accessed | tf_op | source)
XLA Modules:
  0.0 123.2 jit_solution(1133029551912231653)
XLA Ops:
  0.6 73.8 %shard_map.84 = (bf16[128,1536]{1,0:T(8,128)(2,1)}, bf16[128,1536]{1,0:T(8,128)(2,1)}, bf16[128,1536]{1,0:T(8,128)(2,1)}, bf16[128,1536]{1,0:T(8,128)(2,1)}) custom-call(bf16[128,1536]{1,0:T(8,128)(2,1)} %query_ref.1, bf16[128,1536]{1,0:T(8,128)(2,1)} %key_ref.1, bf16[128,1536]{1,0:T(8,128)(2,1)} %value_ref.1, bf16[128,1536]{1,0:T(8,128)(2,1)} %grad_ref.1, ...), custom_call_target="tpu_custom_call" | custom-call | tf_op jit(solution)/shard_map/pallas_call | solution.py:528
  74.4 48.8 %shard_map.85 = (bf16[128,1536]{1,0:T(8,128)(2,1)}, bf16[128,1536]{1,0:T(8,128)(2,1)}, bf16[128,1536]{1,0:T(8,128)(2,1)}, bf16[128,1536]{1,0:T(8,128)(2,1)}) custom-call(bf16[128,1536]{1,0:T(8,128)(2,1)} %get-tuple-element.8.refs_0_, bf16[128,1536]{1,0:T(8,128)(2,1)} %get-tuple-element.9.refs_1_, bf16[128,1536]{1,0:T(8,128)(2,1)} %get-tuple-element.10.refs_2_, ...), custom_call_target="tpu_custom_call" | custom-call | tf_op jit(solution)/shard_map/pallas_call | solution.py:543

commit v4 on v2

--- a/solution.py
+++ b/solution.py
@@ -266,6 +266,8 @@
     dv_sum,
     bias,
     probs,
+    staged,
+    stage_sem,
     in_send,
     in_recv,
     out_send,
@@ -280,6 +282,9 @@
     plane_tokens = tokens // 2
     scaling = HEAD ** (-0.5)
 
+    sources = (key_ref, query_ref, value_ref, grad_ref)
+    landings = (k_all, q_all, v_all, g_all)
+    own_rows = pl.ds(pl.multiple_of(me * BLOCK, BLOCK), BLOCK)
     barrier = pltpu.get_barrier_semaphore()
     for step in range(1, devices):
         pl.semaphore_signal(
@@ -288,11 +293,15 @@
             device_id={"ctx": lax.rem(me + step, devices)},
             device_id_type=pl.DeviceIdType.MESH,
         )
+    for index in range(4):
+        for head in range(HEADS):
+            pltpu.make_async_copy(
+                sources[index].at[:, head * HEAD : (head + 1) * HEAD],
+                staged.at[index, head],
+                stage_sem.at[index],
+            ).start()
+
     pl.semaphore_wait(barrier, devices - 1)
-
-    sources = (key_ref, query_ref, value_ref, grad_ref)
-    landings = (k_all, q_all, v_all, g_all)
-    own_rows = pl.ds(pl.multiple_of(me * BLOCK, BLOCK), BLOCK)
 
     half = me // (devices // 2)
     chips = devices // 2
@@ -300,6 +309,7 @@
 
     def send_inputs(index):
         source, landing = sources[index], landings[index]
+        pltpu.make_async_copy(staged.at[index], staged.at[index], stage_sem.at[index]).wait()
 
         def one(step, carry):
             place = lax.rem(me + step, pairs)
@@ -315,7 +325,7 @@
                 @pl.when(owner != me)
                 def _():
                     pltpu.make_async_remote_copy(
-                        src_ref=source.at[:, columns],
+                        src_ref=staged.at[index, head],
                         dst_ref=landing.at[own_rows, :],
                         send_sem=in_send.at[index],
                         recv_sem=in_recv.at[index],
@@ -342,30 +352,31 @@
     results = (o_all, dq_all, dk_all, dv_all)
     targets = (out_ref, dq_ref, dk_ref, dv_ref)
 
-    def send_row(index, row):
-        result, target = results[index], targets[index]
-        columns = pl.ds(pl.multiple_of(my_head * HEAD, HEAD), HEAD)
-        for column in range(width):
-            for side in (1 - half, half):
-                other = side * (devices // 2) + row * width + column
-                rows = pl.ds(pl.multiple_of(other * BLOCK, BLOCK), BLOCK)
-
-                @pl.when(other != me)
-                def _():
-                    pltpu.make_async_remote_copy(
-                        src_ref=result.at[rows, :],
-                        dst_ref=target.at[:, columns],
-                        send_sem=out_send.at[index],
-                        recv_sem=out_recv.at[index],
-                        device_id={"ctx": other},
-                        device_id_type=pl.DeviceIdType.MESH,
-                    ).start()
-
-                @pl.when(other == me)
-                def _():
-                    pltpu.make_async_copy(
-                        result.at[rows, :], target.at[:, columns], out_recv.at[index]
-                    ).start()
+    def send_rows(indices, rows_here):
+        for index in indices:
+            result, target = results[index], targets[index]
+            for column in range(width):
+                for side in (1 - half, half):
+                    for row in rows_here:
+                        other = side * (devices // 2) + row * width + column
+                        rows = pl.ds(pl.multiple_of(other * BLOCK, BLOCK), BLOCK)
+
+                        @pl.when(other != me)
+                        def _():
+                            pltpu.make_async_remote_copy(
+                                src_ref=result.at[rows, :],
+                                dst_ref=target.at[my_head],
+                                send_sem=out_send.at[index],
+                                recv_sem=out_recv.at[index],
+                                device_id={"ctx": other},
+                                device_id_type=pl.DeviceIdType.MESH,
+                            ).start()
+
+                        @pl.when(other == me)
+                        def _():
+                            pltpu.make_async_copy(
+                                result.at[rows, :], target.at[my_head], out_recv.at[index]
+                            ).start()
 
     def dot(left, right):
         return jnp.dot(left, right, preferred_element_type=jnp.float32)
@@ -393,14 +404,13 @@
                 )
             )
 
-    def finish_keys(row):
+    def finish_keys(rows_here):
         for plane in range(2):
-            start = plane * plane_tokens + row * row_tokens
-            span = slice(start, start + row_tokens)
+            start = plane * plane_tokens + rows_here[0] * row_tokens
+            span = slice(start, start + len(rows_here) * row_tokens)
             dv_all[span, :] = dv_sum[span, :].astype(jnp.bfloat16)
             dk_all[span, :] = (dk_sum[span, :] * scaling).astype(jnp.bfloat16)
-        send_row(3, row)
-        send_row(2, row)
+        send_rows((3, 2), rows_here)
 
     @pl.when(owns)
     def _():
@@ -445,8 +455,8 @@
                 mixed += dot(vt_all[:, first : first + count], weights)
             ot_all[:, start : start + row_tokens] = mixed.astype(jnp.bfloat16)
             o_all[start : start + row_tokens, :] = jnp.transpose(mixed).astype(jnp.bfloat16)
-            if index % 2 == 1:
-                send_row(0, index // 2)
+            if index % 4 == 3:
+                send_rows((0,), (index // 2 - 1, index // 2))
 
         arrived(3)
         flip(g_all, gt_all)
@@ -469,15 +479,14 @@
                 turned += dot(kt_all[:, keys], slopes)
                 dk_sum[keys, :] += dot(slopes, queries)
             dq_all[span, :] = jnp.transpose(turned * scaling).astype(jnp.bfloat16)
-            if index % 2 == 1:
-                row = index // 2
-                send_row(1, row)
-                if row >= 1:
-                    finish_keys(row - 1)
-        finish_keys(TILE_H - 1)
+            if index % 4 == 3:
+                send_rows((1,), (index // 2 - 1, index // 2))
+            if index % 4 == 1 and index > 1:
+                finish_keys((index // 2 - 2, index // 2 - 1))
+        finish_keys((TILE_H - 2, TILE_H - 1))
 
         for index in range(4):
-            sent = sources[index].at[:, : (HEADS - 1) * HEAD]
+            sent = staged.at[index, pl.ds(0, HEADS - 1)]
             pltpu.make_async_copy(sent, sent, in_send.at[index]).wait()
             sent = results[index].at[: (devices - 1) * BLOCK, :]
             pltpu.make_async_copy(sent, sent, out_send.at[index]).wait()
@@ -485,10 +494,30 @@
     @pl.when(jnp.logical_not(owns))
     def _():
         for index in range(4):
-            pltpu.make_async_copy(sources[index], sources[index], in_send.at[index]).wait()
+            pltpu.make_async_copy(staged.at[index], staged.at[index], in_send.at[index]).wait()
 
     for index in range(4):
         pltpu.make_async_copy(targets[index], targets[index], out_recv.at[index]).wait()
+
+
+def place_kernel(*refs):
+    sources, targets, held, in_sem, out_sem = refs[:4], refs[4:8], refs[8], refs[9], refs[10]
+    loads = [
+        pltpu.make_async_copy(sources[index], held.at[index], in_sem.at[index])
+        for index in range(4)
+    ]
+    for load in loads:
+        load.start()
+    for index, load in enumerate(loads):
+        load.wait()
+        for head in range(HEADS):
+            pltpu.make_async_copy(
+                held.at[index, head],
+                targets[index].at[:, head * HEAD : (head + 1) * HEAD],
+                out_sem.at[index],
+            ).start()
+    for index in range(4):
+        pltpu.make_async_copy(held.at[index], held.at[index], out_sem.at[index]).wait()
 
 
 def exchange_sizes(devices):
@@ -504,21 +533,31 @@
     full = lambda *shape: pltpu.VMEM(shape, jnp.float32)
     anywhere = pl.BlockSpec(memory_space=pl.ANY)
     whole = jax.ShapeDtypeStruct(query.shape, query.dtype)
-    return pl.pallas_call(
+    by_head = jax.ShapeDtypeStruct((HEADS, BLOCK, HEAD), query.dtype)
+    landed = pl.pallas_call(
         functools.partial(exchange_kernel, devices),
-        out_shape=(whole,) * 4,
+        out_shape=(by_head,) * 4,
         in_specs=[anywhere] * 4 + [pl.BlockSpec(memory_space=pltpu.VMEM)],
         out_specs=(anywhere,) * 4,
         scratch_shapes=[low(tokens, HEAD)] * 4
         + [low(HEAD, tokens)] * 4
         + [low(tokens, HEAD)] * 4
         + [full(tokens, HEAD)] * 2
-        + [full(devices, tokens), full(*probs_shape)]
-        + [pltpu.SemaphoreType.DMA((4,))] * 4,
+        + [full(devices, tokens), full(*probs_shape), low(4, HEADS, BLOCK, HEAD)]
+        + [pltpu.SemaphoreType.DMA((4,))] * 5,
         compiler_params=pltpu.CompilerParams(
             collective_id=0, has_side_effects=True, vmem_limit_bytes=VMEM_BYTES
         ),
     )(query, key_rows, value, grad_out, kv_slots)
+    return pl.pallas_call(
+        place_kernel,
+        out_shape=(whole,) * 4,
+        in_specs=[anywhere] * 4,
+        out_specs=(anywhere,) * 4,
+        scratch_shapes=[pltpu.VMEM((4,) + by_head.shape, query.dtype)]
+        + [pltpu.SemaphoreType.DMA((4,))] * 2,
+        compiler_params=pltpu.CompilerParams(vmem_limit_bytes=VMEM_BYTES),
+    )(*landed)
 
 
 def fits_exchange(devices, rows):

time: 79.5 us -> 76.7 us (0.965)
  local copies, waits for them, and re-layouts: 4.84 us -> 0 us
  Pallas kernels: 73.8 us -> 75.8 us
    unnamed x10 -> x0, local copies, waits for them, and re-layouts: 4.84 us -> none
    pallas_call x1 -> x2, Pallas kernels: 73.8 us -> 75.8 us  [the longest x1 73.6 us: exchange_body(): pl.pallas_call(functools.partial(exchange_kernel, devices), out_shape=(by...]
where the time goes in v4:
time: 76.7 us; the launch traced here: 76.4 us
  Pallas kernels  75.8 us (99%)
    pallas_call x1, Pallas kernels, exchange_body(): pl.pallas_call(functools.partial(exchange_kernel, devices), out_shape=(by...  73.6 us
    pallas_call x1, Pallas kernels, exchange_body(): pl.pallas_call(place_kernel, out_shape=(whole,) * 4, in_specs=[anywhere]...  2.18 us

profile of v4, /device:TPU:15, one launch (start us, length us, event | category | flops | bytes accessed | tf_op | source)
XLA Modules:
  0.0 76.4 jit_solution(438644858160689958)
XLA Ops:
  0.6 73.6 %shard_map.84 = (bf16[12,128,128]{2,1,0:T(8,128)(2,1)}, bf16[12,128,128]{2,1,0:T(8,128)(2,1)}, bf16[12,128,128]{2,1,0:T(8,128)(2,1)}, bf16[12,128,128]{2,1,0:T(8,128)(2,1)}) custom-call(bf16[128,1536]{1,0:T(8,128)(2,1)} %query_ref.1, bf16[128,1536]{1,0:T(8,128)(2,1)} %key_ref.1, bf16[128,1536]{1,0:T(8,128)(2,1)} %value_ref.1, bf16[128,1536]{1,0:T(8,128)(2,1)} %grad_ref.1, ...), custom_call_target="tpu_custom_call" | custom-call | tf_op jit(solution)/shard_map/pallas_call | solution.py:537
  74.2 2.2 %shard_map.85 = (bf16[128,1536]{1,0:T(8,128)(2,1)}, bf16[128,1536]{1,0:T(8,128)(2,1)}, bf16[128,1536]{1,0:T(8,128)(2,1)}, bf16[128,1536]{1,0:T(8,128)(2,1)}) custom-call(bf16[12,128,128]{2,1,0:T(8,128)(2,1)} %get-tuple-element.8.refs_0_, bf16[12,128,128]{2,1,0:T(8,128)(2,1)} %get-tuple-element.9.refs_1_, bf16[12,128,128]{2,1,0:T(8,128)(2,1)} %get-tuple-element.10.refs_2_, ...), custom_call_target="tpu_custom_call" | custom-call | tf_op jit(solution)/shard_map/pallas_call | solution.py:552

commit v5 on v4

--- a/solution.py
+++ b/solution.py
@@ -15,6 +15,7 @@
 
 head_batch = 4
 masked_score = -1e30
+LOG2_E = 1.4426950408889634
 VMEM_BYTES = 63 * 1024 * 1024
 
 
@@ -266,6 +267,7 @@
     dv_sum,
     bias,
     probs,
+    low_probs,
     staged,
     stage_sem,
     in_send,
@@ -430,7 +432,7 @@
             queries = q_all[start : start + row_tokens, :]
             scores = []
             for offset, first in ranges:
-                part = dot_nt(k_all[first : first + count, :], queries) * scaling
+                part = dot_nt(k_all[first : first + count, :], queries)
                 blocks = count // BLOCK
                 shift = bias[first // BLOCK : first // BLOCK + blocks, start : start + row_tokens]
                 part = part.reshape(blocks, BLOCK, row_tokens) + shift[:, None, :]
@@ -438,20 +440,22 @@
             peak = jnp.maximum(
                 jnp.max(scores[0], axis=0, keepdims=True), jnp.max(scores[1], axis=0, keepdims=True)
             )
-            powers = [jnp.exp(part - peak) for part in scores]
+            powers = [jnp.exp2((part - peak) * (scaling * LOG2_E)) for part in scores]
             total = jnp.sum(powers[0], axis=0, keepdims=True) + jnp.sum(
                 powers[1], axis=0, keepdims=True
             )
             inverse = 1.0 / total
             for (offset, first), part in zip(ranges, powers):
-                probs[index, offset : offset + count, :] = part * inverse
+                part = part * inverse
+                probs[index, offset : offset + count, :] = part
+                low_probs[index, offset : offset + count, :] = part.astype(jnp.bfloat16)
 
         arrived(2)
         flip(v_all, vt_all)
         for index, (start, ranges, count) in enumerate(groups):
             mixed = jnp.zeros((HEAD, row_tokens), jnp.float32)
             for offset, first in ranges:
-                weights = probs[index, offset : offset + count, :].astype(jnp.bfloat16)
+                weights = low_probs[index, offset : offset + count, :]
                 mixed += dot(vt_all[:, first : first + count], weights)
             ot_all[:, start : start + row_tokens] = mixed.astype(jnp.bfloat16)
             o_all[start : start + row_tokens, :] = jnp.transpose(mixed).astype(jnp.bfloat16)
@@ -473,7 +477,7 @@
             for offset, first in ranges:
                 keys = slice(first, first + count)
                 exact = probs[index, offset : offset + count, :]
-                dv_sum[keys, :] += dot(exact.astype(jnp.bfloat16), grads)
+                dv_sum[keys, :] += dot(low_probs[index, offset : offset + count, :], grads)
                 product = dot_nt(v_all[keys, :], grads)
                 slopes = (exact * (product - delta)).astype(jnp.bfloat16)
                 turned += dot(kt_all[:, keys], slopes)
@@ -543,7 +547,7 @@
         + [low(HEAD, tokens)] * 4
         + [low(tokens, HEAD)] * 4
         + [full(tokens, HEAD)] * 2
-        + [full(devices, tokens), full(*probs_shape), low(4, HEADS, BLOCK, HEAD)]
+        + [full(devices, tokens), full(*probs_shape), low(*probs_shape), low(4, HEADS, BLOCK, HEAD)]
         + [pltpu.SemaphoreType.DMA((4,))] * 5,
         compiler_params=pltpu.CompilerParams(
             collective_id=0, has_side_effects=True, vmem_limit_bytes=VMEM_BYTES

time: 76.7 us -> 76.7 us (level)
  no operation moved by 1% of the time
where the time goes in v5:
time: 76.7 us; the launch traced here: 76.4 us
  Pallas kernels  75.8 us (99%)
    pallas_call x1, Pallas kernels, exchange_body(): pl.pallas_call(functools.partial(exchange_kernel, devices), out_shape=(by...  73.6 us
    pallas_call x1, Pallas kernels, exchange_body(): pl.pallas_call(place_kernel, out_shape=(whole,) * 4, in_specs=[anywhere]...  2.18 us

profile of v5, /device:TPU:15, one launch (start us, length us, event | category | flops | bytes accessed | tf_op | source)
XLA Modules:
  0.0 76.4 jit_solution(4793474916607223390)
XLA Ops:
  0.6 73.6 %shard_map.84 = (bf16[12,128,128]{2,1,0:T(8,128)(2,1)}, bf16[12,128,128]{2,1,0:T(8,128)(2,1)}, bf16[12,128,128]{2,1,0:T(8,128)(2,1)}, bf16[12,128,128]{2,1,0:T(8,128)(2,1)}) custom-call(bf16[128,1536]{1,0:T(8,128)(2,1)} %query_ref.1, bf16[128,1536]{1,0:T(8,128)(2,1)} %key_ref.1, bf16[128,1536]{1,0:T(8,128)(2,1)} %value_ref.1, bf16[128,1536]{1,0:T(8,128)(2,1)} %grad_ref.1, ...), custom_call_target="tpu_custom_call" | custom-call | tf_op jit(solution)/shard_map/pallas_call | solution.py:541
  74.2 2.2 %shard_map.85 = (bf16[128,1536]{1,0:T(8,128)(2,1)}, bf16[128,1536]{1,0:T(8,128)(2,1)}, bf16[128,1536]{1,0:T(8,128)(2,1)}, bf16[128,1536]{1,0:T(8,128)(2,1)}) custom-call(bf16[12,128,128]{2,1,0:T(8,128)(2,1)} %get-tuple-element.8.refs_0_, bf16[12,128,128]{2,1,0:T(8,128)(2,1)} %get-tuple-element.9.refs_1_, bf16[12,128,128]{2,1,0:T(8,128)(2,1)} %get-tuple-element.10.refs_2_, ...), custom_call_target="tpu_custom_call" | custom-call | tf_op jit(solution)/shard_map/pallas_call | solution.py:556
